TPU v7x, 128 devices: a whole 4x4x4 slice. The times are simulated.
128 devices in a mesh: role: 2 (over y_hi), dev: 64 (over z, x, y_lo, core).
Axes of the slice: x: 4, y: 4 (y_hi: 2, y_lo: 2; y = y_hi * 2 + y_lo), z: 4, core: 2. Of those that a mesh axis runs over, the one named last changes fastest.
Arguments:
- tokens: bfloat16 [65536, 1024], P(('role', 'dev')), may hold values from -6 to 6
- expert_ids: int32 [65536, 1], P(('role', 'dev')), may hold values from 0 to 127; in each aligned block of 512 rows (0 to 511, 512 to 1023, ...) at most 8 rows name the same one
- w_qkv: bfloat16 [1024, 3072], P(('role', 'dev')), may hold values from -2 to 2
- w_attn_out: bfloat16 [1024, 1024], P(('role', 'dev')), may hold values from -0.1875 to 0.1875
- gain_attn: bfloat16 [1024], replicated, may hold values from 0.5 to 1.5
- gain_expert: bfloat16 [1024], replicated, may hold values from 0.5 to 1.5
- router: bfloat16 [1024, 128], replicated, may hold values from -0.375 to 0.375
- expert_in: bfloat16 [128, 1024, 2816], P(('role', 'dev')), may hold values from -0.1875 to 0.1875
- expert_out: bfloat16 [128, 2816, 1024], P(('role', 'dev')), may hold values from -0.109375 to 0.109375
- capacity: int32 [128], replicated, may hold values from 256 to 1023
- swap_list: int32 [32], replicated, may hold values from 0 to 63, as said below
Outputs:
- mixed: bfloat16 [65536, 1024], P(('role', 'dev'))
Inputs may be any that keep to these rules, and one draw needn't show every extreme that they name: `expert_ids`: in the rows of one device no expert is named more than 8 times, a bound that some block reaches. `swap_list`: entries are distinct.
All inputs are finite; a program needn't handle non-finite values.
Results may differ from a plain program's by a relative error of at most 0.0052.
Values may be sent and summed in bfloat16 or wider, within the bound.
A program may use at most 128 MiB of HBM per device.

v0:
```python
import jax
import jax.numpy as jnp
from jax import lax
from jax.sharding import PartitionSpec as P

HEADS = 16


def rms_scale(values, gain_vector):
    mean_sq = jnp.mean(values * values, axis=-1, keepdims=True)
    return values * lax.rsqrt(mean_sq + 1e-06) * gain_vector.astype(jnp.float32)


def self_attend(qkv_rows, head_count):
    row_count = qkv_rows.shape[0]
    model_width = qkv_rows.shape[1] // 3
    head_size = model_width // head_count
    queries = qkv_rows[:, :model_width].reshape(row_count, head_count, head_size)
    keys_all = qkv_rows[:, model_width : 2 * model_width].reshape(row_count, head_count, head_size)
    values = qkv_rows[:, 2 * model_width :].reshape(row_count, head_count, head_size)
    scores = jnp.einsum(
        "shd,thd->hst", queries, keys_all, preferred_element_type=jnp.float32
    ) * head_size ** (-0.5)
    row_max = jnp.max(scores, axis=-1, keepdims=True)
    weights = jnp.exp(scores - row_max)
    soft_weights = (weights / jnp.sum(weights, axis=-1, keepdims=True)).astype(jnp.bfloat16)
    context = jnp.einsum("hst,thd->shd", soft_weights, values, preferred_element_type=jnp.float32)
    return context.reshape(row_count, model_width).astype(jnp.bfloat16)


def shards(
    tokens,
    expert_ids,
    w_qkv,
    w_attn_out,
    gain_attn,
    gain_expert,
    router,
    expert_in,
    expert_out,
    capacity,
    swap_list,
):
    seq_len, model_width = tokens.shape
    experts_all = router.shape[1]
    dev_count = lax.axis_size("dev")
    me = lax.axis_index("role") * dev_count + lax.axis_index("dev")
    chosen = expert_ids[:, 0]
    expert_range = jnp.arange(experts_all, dtype=jnp.int32)
    match = chosen[:, None] == expert_range[None, :]
    counts = jnp.sum(match.astype(jnp.float32), axis=0)
    row_share = w_attn_out.shape[0]
    beside = jnp.broadcast_to(counts.astype(jnp.bfloat16)[None, :], (row_share, experts_all))
    w_qkv_all = lax.all_gather(w_qkv, ("role", "dev"), axis=0, tiled=True)
    w_out_counts = lax.all_gather(
        jnp.concatenate([w_attn_out, beside], axis=1), ("role", "dev"), axis=0, tiled=True
    )
    w_out_all = w_out_counts[:, :model_width]
    counts_all = w_out_counts[:, model_width:].astype(jnp.float32)
    residual = tokens.astype(jnp.float32)
    normed = rms_scale(residual, gain_attn).astype(jnp.bfloat16)
    qkv_rows = jnp.dot(normed, w_qkv_all, preferred_element_type=jnp.float32).astype(jnp.bfloat16)
    context = self_attend(qkv_rows, HEADS)
    attended = jnp.dot(context, w_out_all, preferred_element_type=jnp.float32)
    hidden = residual + attended
    normed_ffn = rms_scale(hidden, gain_expert).astype(jnp.bfloat16)
    logits = jnp.dot(normed_ffn, router, preferred_element_type=jnp.float32)
    gate = jax.nn.sigmoid(jnp.sum(jnp.where(match, logits, 0.0), axis=1))
    gathered_row = jnp.arange(w_out_counts.shape[0], dtype=jnp.int32)
    first_of_lower = (gathered_row % row_share == 0) & (gathered_row < me * row_share)
    before = jnp.sum(jnp.where(first_of_lower[:, None], counts_all, 0.0), axis=0).astype(jnp.int32)
    row_ids = lax.broadcasted_iota(jnp.int32, (seq_len, seq_len), 0)
    col_ids = lax.broadcasted_iota(jnp.int32, (seq_len, seq_len), 1)
    strict_lower = (col_ids < row_ids).astype(jnp.bfloat16)
    rank_table = jnp.dot(
        strict_lower, match.astype(jnp.bfloat16), preferred_element_type=jnp.float32
    )
    local_rank = jnp.sum(jnp.where(match, rank_table, 0.0), axis=1).astype(jnp.int32)
    flagged = jnp.any(swap_list[:, None] == (expert_range % dev_count)[None, :], axis=0)
    location = jnp.where(
        flagged,
        (1 - expert_range // dev_count) * dev_count + expert_range % dev_count,
        expert_range,
    )
    cap_expert = jnp.sum(
        jnp.where(location[:, None] == expert_range[None, :], capacity[None, :], 0), axis=1
    )
    room = jnp.sum(jnp.where(match, (cap_expert - before)[None, :], 0), axis=1)
    kept = local_rank < room
    slot_rows = max(2, 2 * seq_len // experts_all)
    slot_index = chosen * slot_rows + local_rank
    buffer = (
        jnp.zeros((experts_all * slot_rows, model_width), jnp.bfloat16)
        .at[slot_index]
        .set(normed_ffn)
    )
    buffer = buffer.reshape(experts_all, slot_rows, model_width)
    received = lax.all_to_all(buffer, ("role", "dev"), split_axis=0, concat_axis=0, tiled=True)
    flat_rows = received.reshape(-1, model_width)
    activ = jnp.maximum(
        jnp.dot(flat_rows, expert_in[0], preferred_element_type=jnp.float32), 0.0
    ).astype(jnp.bfloat16)
    produced = jnp.dot(activ, expert_out[0], preferred_element_type=jnp.float32).astype(
        jnp.bfloat16
    )
    returned = lax.all_to_all(
        produced.reshape(received.shape), ("role", "dev"), split_axis=0, concat_axis=0, tiled=True
    )
    picked = returned.reshape(-1, model_width)[slot_index].astype(jnp.float32)
    mixed = hidden + jnp.where(kept, gate, 0.0)[:, None] * picked
    return mixed.astype(jnp.bfloat16)


def solution(mesh):
    return jax.shard_map(
        shards,
        mesh=mesh,
        in_specs=(
            P(("role", "dev"), None),
            P(("role", "dev"), None),
            P(("role", "dev"), None),
            P(("role", "dev"), None),
            P(),
            P(),
            P(),
            P(("role", "dev"), None, None),
            P(("role", "dev"), None, None),
            P(),
            P(),
        ),
        out_specs=P(("role", "dev"), None),
        check_vma=False,
    )
```

profile of v0, /device:TPU:1, one launch (start us, length us, event | category | flops | bytes accessed | tf_op | source)
XLA Modules:
  0.0 543.9 jit_solution(13328983588783734657)
XLA Ops:
  6.5 0.9 convert_reduce_fusion
  7.5 1.3 pad_maximum_fusion
  8.9 0.7 all-gather.3.cloned.1.call-update
  9.6 0.7 convert_element_type.81
  10.3 0.7 convert_element_type.93
  11.0 0.7 compare_reduce_fusion
  11.7 0.8 select_reduce_fusion.2
  12.5 1.1 fusion.30
  13.6 1.5 fusion.13
  15.1 192.9 %all-gather.5.cloned.1.call-done = bf16[1024,1152]{1,0:T(8,128)(2,1)} async-done(((bf16[8,1152]{1,0:T(8,128)(2,1)}), bf16[1024,1152]{1,0:T(8,128)(2,1)}) %all-gather.5.cloned.1.call-update) | async-done | bytes 2359312 | tf_op jit(solution)/shard_map/all_gather | solution.py:55
  208.1 1.2 select_reduce_fusion
  209.4 200.2 %all-gather.3.cloned.1.call-done = bf16[1024,3072]{1,0:T(8,128)(2,1)} async-done(((bf16[8,3072]{1,0:T(8,128)(2,1)}), bf16[1024,3072]{1,0:T(8,128)(2,1)}) %all-gather.3.cloned.1.call-update) | async-done | bytes 6291472 | tf_op jit(solution)/shard_map/all_gather | solution.py:54
  409.6 6.6 %convolution_convert_fusion = bf16[512,3072]{1,0:T(8,128)(2,1)S(1)} fusion(bf16[1024,3072]{1,0:T(8,128)(2,1)} %all-gather.3.cloned.1.call-done, bf16[512,1024]{1,0:T(8,128)(2,1)S(1)} %copy-done.2, f32[1024]{0:T(1024)S(1)} %convert_element_type.81, f32[512]{0:T(512)S(1)} %add_rsqrt_fusion.1), kind=kOutput, calls=%fused_computation.13 | convolution fusion | flops 3224895488 | bytes 10491904 | tf_op jit(solution)/shard_map/dot_general | solution.py:62
  416.5 1.3 copy.20
  418.9 8.9 %fusion.49 = (f32[16,512]{1,0:T(8,128)S(1)}, f32[16,512,512]{1,2,0:T(8,128)}) fusion(bf16[512,16,64]{0,2,1:T(8,128)(2,1)S(1)} %bitcast.42, bf16[512,16,64]{0,2,1:T(8,128)(2,1)S(1)} %bitcast.43), kind=kOutput, calls=%fused_computation.73 | convolution fusion | flops 549454336 | bytes 18907136 | tf_op jit(solution)/shard_map/sub | solution.py:25
  427.9 7.6 %fusion.28 = bf16[16,64,512]{2,1,0:T(8,128)(2,1)S(1)} fusion(bf16[512,16,64]{0,2,1:T(8,128)(2,1)S(1)} %bitcast.41, f32[16,512,512]{1,2,0:T(8,128)} %get-tuple-element.11, f32[16,512]{1,0:T(8,128)S(1)} %get-tuple-element.10), kind=kOutput, calls=%fused_computation.28 | convolution fusion | flops 545783808 | bytes 18907136 | tf_op jit(solution)/shard_map/hst,thd->shd/dot_general | solution.py:27
  435.5 1.4 multiply_reduce_fusion.1
  437.5 4.2 scatter_custom_fusion
  441.7 37.2 %all_to_all.10 = bf16[128,8,1024]{2,1,0:T(8,128)(2,1)S(1)} all-to-all(bf16[128,8,1024]{2,1,0:T(8,128)(2,1)} %bitcast.40), channel_id=1, replica_groups=mesh['role'=2,'dev'=64] {'role','dev'}, dimensions={0} | all-to-all | bytes 4194304 | tf_op jit(solution)/shard_map/all_to_all | solution.py:98
  478.9 17.7 %convert_bitcast_fusion = bf16[128,8,1024]{2,1,0:T(8,128)(2,1)} fusion(bf16[1,2816,1024]{2,1,0:T(8,128)(2,1)} %param.19, bf16[1,1024,2816]{2,1,0:T(8,128)(2,1)} %param.18, bf16[128,8,1024]{2,1,0:T(8,128)(2,1)S(1)} %all_to_all.10), kind=kOutput, calls=%fused_computation.25 | convolution fusion | flops 11817975808 | bytes 15728640 | tf_op jit(solution)/shard_map/dot_general | solution.py:103
  496.6 5.4 all-to-all-start.1
  502.0 30.1 %all-to-all-done.1 = bf16[128,8,1024]{2,1,0:T(8,128)(2,1)S(1)} async-done(((bf16[128,8,1024]{2,1,0:T(8,128)(2,1)}), bf16[128,8,1024]{2,1,0:T(8,128)(2,1)S(1)}, u32[]{:S(2)}, u32[]{:S(2)}) %all-to-all-start.1) | async-done | bytes 2097184 | tf_op jit(solution)/shard_map/all_to_all | solution.py:106
  532.1 2.0 gather_fusion
  534.2 2.9 add_convert_fusion
  (32 shorter events, 2.3 us)
Async XLA Ops:
  6.5 430.3 %copy-start = (bf16[1024,128]{1,0:T(8,128)(2,1)S(1)}, bf16[1024,128]{1,0:T(8,128)(2,1)}, u32[]{:S(2)}) copy-start(bf16[1024,128]{1,0:T(8,128)(2,1)} %param.17) | copy-start | bytes 786436
  6.5 202.7 %copy-start.5 = (s32[512,1]{0,1:T(1,128)S(1)}, s32[512,1]{0,1:T(1,128)}, u32[]{:S(2)}) copy-start(s32[512,1]{0,1:T(1,128)} %param.12) | copy-start | bytes 6148
  6.5 403.0 %copy-start.2 = (bf16[512,1024]{1,0:T(8,128)(2,1)S(1)}, bf16[512,1024]{1,0:T(8,128)(2,1)}, u32[]{:S(2)}) copy-start(bf16[512,1024]{1,0:T(8,128)(2,1)} %param.11) | copy-start | bytes 3145732
  6.5 201.5 %all-gather.5.cloned.1.call-start = ((), (), s32[]{:S(2)}) async-start(), calls=%async_computation.3 | async-start | bytes 2377728 | tf_op jit(solution)/shard_map/all_gather | solution.py:55
  8.8 400.8 %all-gather.3.cloned.1.call-start = ((), (), s32[]{:S(2)}) async-start(), calls=%async_computation.2 | async-start | bytes 6340608 | tf_op jit(solution)/shard_map/all_gather | solution.py:54
  418.9 8.9 %copy-start.4 = (bf16[512,1024]{0,1:T(8,128)(2,1)S(1)}, bf16[512,1024]{0,1:T(8,128)(2,1)}, u32[]{:S(2)}) copy-start(bf16[512,1024]{0,1:T(8,128)(2,1)} %copy.20) | copy-start | bytes 3145732
  427.8 7.6 %copy-start.3 = (bf16[512,1024]{1,0:T(8,128)(2,1)S(1)}, bf16[512,1024]{1,0:T(8,128)(2,1)}, u32[]{:S(2)}) copy-start(bf16[512,1024]{1,0:T(8,128)(2,1)} %param.11) | copy-start | bytes 3145732
  427.9 7.6 %copy-start.6 = (bf16[1024,1152]{1,0:T(8,128)(2,1)S(1)}, bf16[1024,1152]{1,0:T(8,128)(2,1)}, u32[]{:S(2)}) copy-start(bf16[1024,1152]{1,0:T(8,128)(2,1)} %all-gather.5.cloned.1.call-done) | copy-start | bytes 7077892
  436.8 4.9 copy-start.1
  496.6 35.6 %all-to-all-start.1 = ((bf16[128,8,1024]{2,1,0:T(8,128)(2,1)}), bf16[128,8,1024]{2,1,0:T(8,128)(2,1)S(1)}, u32[]{:S(2)}, u32[]{:S(2)}) async-start(bf16[128,8,1024]{2,1,0:T(8,128)(2,1)} %convert_bitcast_fusion), calls=%async_computation.1 | async-start | bytes 4194304 | tf_op jit(solution)/shard_map/all_to_all | solution.py:106
Sparse Core Ops, SparseCore 0:
  9.1 198.9 all-gather.4
  209.8 199.7 all-gather.2
where the time goes:
time: 544 us
  waiting for transfers between devices  424 us (78%)
  matrix products  43.8 us (8%)
  blocking collectives  37.2 us (7%)
  other arithmetic  15.1 us (3%)
  between operations  13.6 us (2%)
  starting transfers between devices  5.47 us (1%)
    all_gather x1, waiting for transfers between devices, shards(): w_qkv_all = lax.all_gather(w_qkv, ('role', 'dev'), axis=0, tiled=True)  200 us
    all_gather x1, waiting for transfers between devices, shards(): lax.all_gather(jnp.concatenate([w_attn_out, beside], axis=1), ('role', 'd...  193 us
    all_to_all x1, blocking collectives, shards(): lax.all_to_all(buffer, ('role', 'dev'), split_axis=0, concat_axis=0, tile...  37.2 us
    all_to_all x1, waiting for transfers between devices, shards(): lax.all_to_all(produced.reshape(received.shape), ('role', 'dev'), split_a...  30.1 us
    dot_general x1, matrix products, shards(): jnp.dot(activ, expert_out[0], preferred_element_type=jnp.float32)  17.7 us
  transfers between devices with their start and end apart: 3, of which 3 were waited for; matrix products, arithmetic and copies ran while one was open for 1% of the time, Pallas kernels for 0%

commit v1 on v0

--- a/solution.py
+++ b/solution.py
@@ -52,8 +52,16 @@
     row_share = w_attn_out.shape[0]
     beside = jnp.broadcast_to(counts.astype(jnp.bfloat16)[None, :], (row_share, experts_all))
     w_qkv_all = lax.all_gather(w_qkv, ("role", "dev"), axis=0, tiled=True)
-    w_out_counts = lax.all_gather(
-        jnp.concatenate([w_attn_out, beside], axis=1), ("role", "dev"), axis=0, tiled=True
+    w_out_counts = jnp.concatenate(
+        lax.all_to_all(
+            jnp.stack(
+                [jnp.concatenate([w_attn_out, beside], axis=1)] * lax.axis_size(("role", "dev"))
+            ),
+            ("role", "dev"),
+            0,
+            0,
+        ),
+        axis=0,
     )
     w_out_all = w_out_counts[:, :model_width]
     counts_all = w_out_counts[:, model_width:].astype(jnp.float32)

time: 544 us -> 367 us (0.67)
  waiting for transfers between devices: 424 us -> 238 us
  starting transfers between devices: 5.47 us -> 16.9 us
    all_gather x1 -> x0, waiting for transfers between devices: 193 us -> none  [shards(): lax.all_gather(jnp.concatenate([w_attn_out, beside], axis=1), ('role', 'd...]
    all_to_all x0 -> x1, waiting for transfers between devices: none -> 31.1 us  [shards(): lax.all_to_all(jnp.stack([jnp.concatenate([w_attn_out, beside], axis=1)]...]
    all_gather x1, waiting for transfers between devices: 200 us -> 176 us  [shards(): w_qkv_all = lax.all_gather(w_qkv, ('role', 'dev'), axis=0, tiled=True)]
    all_to_all x0 -> x1, starting transfers between devices: none -> 11.5 us  [shards(): lax.all_to_all(jnp.stack([jnp.concatenate([w_attn_out, beside], axis=1)]...]
  transfers between devices with their start and end apart: 3 -> 3, of which waited for: 3 -> 3; matrix products, arithmetic and copies ran while one was open for 1% -> 2% of each run, Pallas kernels for 0% -> 0%
where the time goes in v1:
time: 367 us; the launch traced here: 366 us
  waiting for transfers between devices  238 us (65%)
  matrix products  43 us (12%)
  blocking collectives  37.8 us (10%)
  starting transfers between devices  16.9 us (5%)
  between operations  13.6 us (4%)
  other arithmetic  10.8 us (3%)
  local copies, waits for them, and re-layouts  6.43 us (2%)
    all_gather x1, waiting for transfers between devices, shards(): w_qkv_all = lax.all_gather(w_qkv, ('role', 'dev'), axis=0, tiled=True)  176 us
    all_to_all x1, blocking collectives, shards(): lax.all_to_all(buffer, ('role', 'dev'), split_axis=0, concat_axis=0, tile...  37.8 us
    all_to_all x1, waiting for transfers between devices, shards(): lax.all_to_all(jnp.stack([jnp.concatenate([w_attn_out, beside], axis=1)]...  31.1 us
    all_to_all x1, waiting for transfers between devices, shards(): lax.all_to_all(produced.reshape(received.shape), ('role', 'dev'), split_a...  30.1 us
    dot_general x1, matrix products, shards(): jnp.dot(activ, expert_out[0], preferred_element_type=jnp.float32)  17.7 us
    all_to_all x1, starting transfers between devices, shards(): lax.all_to_all(jnp.stack([jnp.concatenate([w_attn_out, beside], axis=1)]...  11.5 us
    sub x1, matrix products, self_attend(): weights = jnp.exp(scores - row_max)  8.9 us
    dot_general x1, matrix products, self_attend(): jnp.einsum('hst,thd->shd', soft_weights, values, preferred_element_type=j...  7.5 us
  transfers between devices with their start and end apart: 3, of which 3 were waited for; matrix products, arithmetic and copies ran while one was open for 2% of the time, Pallas kernels for 0%

profile of v1, /device:TPU:1, one launch (start us, length us, event | category | flops | bytes accessed | tf_op | source)
XLA Modules:
  0.0 366.2 jit_solution(9466304198877491365)
XLA Ops:
  6.5 0.7 all-gather.2.cloned.1.call-update
  7.3 0.8 convert_reduce_fusion
  8.1 0.7 pad_maximum_fusion
  8.8 1.6 stack.2
  10.4 11.5 %all-to-all-start = ((bf16[128,8,1152]{2,1,0:T(8,128)(2,1)}), bf16[128,8,1152]{2,1,0:T(8,128)(2,1)S(1)}, u32[]{:S(2)}, u32[]{:S(2)}) async-start(bf16[128,8,1152]{2,1,0:T(8,128)(2,1)} %stack.2), calls=%async_computation | async-start | bytes 4718592 | tf_op jit(solution)/shard_map/all_to_all | solution.py:56
  22.6 1.5 fusion.13
  24.1 31.1 %all-to-all-done = bf16[128,8,1152]{2,1,0:T(8,128)(2,1)S(1)} async-done(((bf16[128,8,1152]{2,1,0:T(8,128)(2,1)}), bf16[128,8,1152]{2,1,0:T(8,128)(2,1)S(1)}, u32[]{:S(2)}, u32[]{:S(2)}) %all-to-all-start) | async-done | bytes 2359328 | tf_op jit(solution)/shard_map/all_to_all | solution.py:56
  55.6 175.7 %all-gather.2.cloned.1.call-done = bf16[1024,3072]{1,0:T(8,128)(2,1)} async-done(((bf16[8,3072]{1,0:T(8,128)(2,1)}), bf16[1024,3072]{1,0:T(8,128)(2,1)}) %all-gather.2.cloned.1.call-update) | async-done | bytes 6291472 | tf_op jit(solution)/shard_map/all_gather | solution.py:54
  231.4 6.6 %convolution_convert_fusion = bf16[512,3072]{1,0:T(8,128)(2,1)S(1)} fusion(bf16[1024,3072]{1,0:T(8,128)(2,1)} %all-gather.2.cloned.1.call-done, bf16[512,1024]{1,0:T(8,128)(2,1)} %param.11, f32[1024]{0:T(1024)S(1)} %convert_element_type.81, f32[512]{0:T(512)S(1)} %add_rsqrt_fusion.1), kind=kOutput, calls=%fused_computation.13 | convolution fusion | flops 3224895488 | bytes 10491904 | tf_op jit(solution)/shard_map/dot_general | solution.py:70
  238.0 0.3 fusion.48
  238.3 1.3 copy.20
  239.7 0.5 copy.21
  240.2 0.5 copy.22
  240.8 8.9 %fusion.49 = (f32[16,512]{1,0:T(8,128)S(1)}, f32[16,512,512]{1,2,0:T(8,128)}) fusion(bf16[512,16,64]{0,2,1:T(8,128)(2,1)S(1)} %bitcast.45, bf16[512,16,64]{0,2,1:T(8,128)(2,1)S(1)} %bitcast.46), kind=kOutput, calls=%fused_computation.73 | convolution fusion | flops 549454336 | bytes 18907136 | tf_op jit(solution)/shard_map/sub | solution.py:25
  249.7 7.5 %fusion.28 = bf16[16,64,512]{2,1,0:T(8,128)(2,1)S(1)} fusion(bf16[512,16,64]{0,2,1:T(8,128)(2,1)S(1)} %bitcast.44, f32[16,512,512]{1,2,0:T(8,128)} %get-tuple-element.11, f32[16,512]{1,0:T(8,128)S(1)} %get-tuple-element.10), kind=kOutput, calls=%fused_computation.28 | convolution fusion | flops 545783808 | bytes 18907136 | tf_op jit(solution)/shard_map/hst,thd->shd/dot_general | solution.py:27
  257.2 1.4 multiply_reduce_fusion.1
  258.6 0.6 fusion.29
  259.2 4.2 %scatter_custom_fusion = bf16[1024,1024]{1,0:T(8,128)(2,1)} fusion(s32[512]{0:T(512)S(1)} %bitcast.51, bf16[]{:T(256)} %constant.86.clone.1, f32[512,1024]{1,0:T(8,128)S(1)} %get-tuple-element.13, f32[1024]{0:T(1024)S(1)} %convert_element_type.93, f32[512]{0:T(512)S(1)} %add_rsqrt_fusion), kind=kCustom, calls=%fused_computation.33 | custom fusion | flops 1572864 | bytes 4200450 | tf_op jit(solution)/shard_map/scatter | solution.py:103
  263.4 37.8 %all_to_all.15 = bf16[128,8,1024]{2,1,0:T(8,128)(2,1)S(1)} all-to-all(bf16[128,8,1024]{2,1,0:T(8,128)(2,1)} %bitcast.41), channel_id=1, replica_groups=mesh['role'=2,'dev'=64] {'role','dev'}, dimensions={0} | all-to-all | bytes 4194304 | tf_op jit(solution)/shard_map/all_to_all | solution.py:106
  301.2 17.7 %convert_bitcast_fusion = bf16[128,8,1024]{2,1,0:T(8,128)(2,1)} fusion(bf16[1,2816,1024]{2,1,0:T(8,128)(2,1)} %param.19, bf16[1,1024,2816]{2,1,0:T(8,128)(2,1)} %param.18, bf16[128,8,1024]{2,1,0:T(8,128)(2,1)S(1)} %all_to_all.15), kind=kOutput, calls=%fused_computation.25 | convolution fusion | flops 11817975808 | bytes 15728640 | tf_op jit(solution)/shard_map/dot_general | solution.py:111
  318.9 5.4 %all-to-all-start.2 = ((bf16[128,8,1024]{2,1,0:T(8,128)(2,1)}), bf16[128,8,1024]{2,1,0:T(8,128)(2,1)S(1)}, u32[]{:S(2)}, u32[]{:S(2)}) async-start(bf16[128,8,1024]{2,1,0:T(8,128)(2,1)} %convert_bitcast_fusion), calls=%async_computation.2 | async-start | bytes 4194304 | tf_op jit(solution)/shard_map/all_to_all | solution.py:114
  324.3 30.1 %all-to-all-done.2 = bf16[128,8,1024]{2,1,0:T(8,128)(2,1)S(1)} async-done(((bf16[128,8,1024]{2,1,0:T(8,128)(2,1)}), bf16[128,8,1024]{2,1,0:T(8,128)(2,1)S(1)}, u32[]{:S(2)}, u32[]{:S(2)}) %all-to-all-start.2) | async-done | bytes 2097184 | tf_op jit(solution)/shard_map/all_to_all | solution.py:114
  354.4 2.0 gather_fusion
  356.5 2.9 add_convert_fusion
  (40 shorter events, 1.0 us)
Async XLA Ops:
  6.5 252.1 %copy-start = (bf16[1024,128]{1,0:T(8,128)(2,1)S(1)}, bf16[1024,128]{1,0:T(8,128)(2,1)}, u32[]{:S(2)}) copy-start(bf16[1024,128]{1,0:T(8,128)(2,1)} %param.17) | copy-start | bytes 786436
  6.5 224.8 %all-gather.2.cloned.1.call-start = ((), (), s32[]{:S(2)}) async-start(), calls=%async_computation.3 | async-start | bytes 6340608 | tf_op jit(solution)/shard_map/all_gather | solution.py:54
  10.4 11.5 %copy-start.7 = (bf16[1024]{0:T(1024)(128)(2,1)S(1)}, bf16[1024]{0:T(1024)(128)(2,1)}, u32[]{:S(2)}) copy-start(bf16[1024]{0:T(1024)(128)(2,1)} %param.15) | copy-start | bytes 6148
  10.4 11.6 %copy-start.8 = (bf16[1024]{0:T(1024)(128)(2,1)S(1)}, bf16[1024]{0:T(1024)(128)(2,1)}, u32[]{:S(2)}) copy-start(bf16[1024]{0:T(1024)(128)(2,1)} %param.16) | copy-start | bytes 6148
  10.4 11.6 %copy-start.9 = (s32[32]{0:T(128)S(1)}, s32[32]{0:T(128)}, u32[]{:S(2)}) copy-start(s32[32]{0:T(128)} %param.21) | copy-start | bytes 388
  10.4 11.7 %copy-start.10 = (s32[128]{0:T(128)S(1)}, s32[128]{0:T(128)}, u32[]{:S(2)}) copy-start(s32[128]{0:T(128)} %param.20) | copy-start | bytes 1540
  10.4 11.9 %copy-start.6 = (s32[512,1]{0,1:T(1,128)S(1)}, s32[512,1]{0,1:T(1,128)}, u32[]{:S(2)}) copy-start(s32[512,1]{0,1:T(1,128)} %param.12) | copy-start | bytes 6148
  10.4 44.9 %all-to-all-start = ((bf16[128,8,1152]{2,1,0:T(8,128)(2,1)}), bf16[128,8,1152]{2,1,0:T(8,128)(2,1)S(1)}, u32[]{:S(2)}, u32[]{:S(2)}) async-start(bf16[128,8,1152]{2,1,0:T(8,128)(2,1)} %stack.2), calls=%async_computation | async-start | bytes 4718592 | tf_op jit(solution)/shard_map/all_to_all | solution.py:56
  55.3 176.1 %copy-start.2 = (bf16[128,8,1152]{2,1,0:T(8,128)(2,1)}, bf16[128,8,1152]{2,1,0:T(8,128)(2,1)S(1)}, u32[]{:S(2)}) copy-start(bf16[128,8,1152]{2,1,0:T(8,128)(2,1)S(1)} %all-to-all-done) | copy-start | bytes 7077892
  240.8 8.9 %copy-start.5 = (bf16[512,1024]{0,1:T(8,128)(2,1)S(1)}, bf16[512,1024]{0,1:T(8,128)(2,1)}, u32[]{:S(2)}) copy-start(bf16[512,1024]{0,1:T(8,128)(2,1)} %copy.20) | copy-start | bytes 3145732
  249.7 7.5 %copy-start.3 = (bf16[128,8,1152]{2,1,0:T(8,128)(2,1)S(1)}, bf16[128,8,1152]{2,1,0:T(8,128)(2,1)}, u32[]{:S(2)}) copy-start(bf16[128,8,1152]{2,1,0:T(8,128)(2,1)} %copy-done.2) | copy-start | bytes 7077892
  249.7 7.5 %copy-start.4 = (bf16[512,1024]{1,0:T(8,128)(2,1)S(1)}, bf16[512,1024]{1,0:T(8,128)(2,1)}, u32[]{:S(2)}) copy-start(bf16[512,1024]{1,0:T(8,128)(2,1)} %param.11) | copy-start | bytes 3145732
  258.6 4.8 %copy-start.1 = (f32[512,1024]{1,0:T(8,128)}, f32[512,1024]{1,0:T(8,128)S(1)}, u32[]{:S(2)}) copy-start(f32[512,1024]{1,0:T(8,128)S(1)} %get-tuple-element.13) | copy-start | bytes 6291460
  318.9 35.6 %all-to-all-start.2 = ((bf16[128,8,1024]{2,1,0:T(8,128)(2,1)}), bf16[128,8,1024]{2,1,0:T(8,128)(2,1)S(1)}, u32[]{:S(2)}, u32[]{:S(2)}) async-start(bf16[128,8,1024]{2,1,0:T(8,128)(2,1)} %convert_bitcast_fusion), calls=%async_computation.2 | async-start | bytes 4194304 | tf_op jit(solution)/shard_map/all_to_all | solution.py:114
Sparse Core Ops, SparseCore 0:
  9.1 222.2 all-gather.1
